TPU v7x, 128 devices: a whole 4x4x4 slice. The times are simulated.
128 devices in a mesh: dp: 4 (over y), mp: 32 (over x, z, core).
Axes of the slice: x: 4, y: 4, z: 4, core: 2. Of those that a mesh axis runs over, the one named last changes fastest.
Arguments:
- residual_in: bfloat16 [512, 3584], P('dp', 'mp'), may hold values from -6 to 6
- pre_gain: float32 [3584], replicated, may hold values from 0.5 to 1.5
- post_gain: float32 [3584], replicated, may hold values from 0.5 to 1.5
- w_gate: bfloat16 [3584, 14336], P(None, 'mp'), may hold values from -0.09375 to 0.09375
- w_up: bfloat16 [3584, 14336], P(None, 'mp'), may hold values from -0.09375 to 0.09375
- w_down: bfloat16 [14336, 3584], P('mp'), may hold values from -0.046875 to 0.046875
- w_enc: bfloat16 [3584, 65536], P(None, ('dp', 'mp')), may hold values from -0.09375 to 0.09375
- b_enc: float32 [65536], P(('dp', 'mp')), may hold values from -2.5 to 2.5
- threshold: float32 [65536], P(('dp', 'mp')), may hold values from 0.1 to 1
- w_dec: bfloat16 [65536, 3584], P(('dp', 'mp')), may hold values from -0.0234375 to 0.0234375
- b_dec: float32 [3584], replicated, may hold values from -1.5 to 1.5
Outputs:
- loss_value: float32 [], replicated
- d_w_enc: bfloat16 [3584, 65536], P(None, ('dp', 'mp'))
- d_w_dec: bfloat16 [65536, 3584], P(('dp', 'mp'))
- d_b_enc: float32 [65536], P(('dp', 'mp'))
- d_threshold: float32 [65536], P(('dp', 'mp'))
- d_b_dec: float32 [3584], replicated
All inputs are finite; a program needn't handle non-finite values.
Results may differ from a plain program's by a relative error of at most 0.014.
The roundings to bfloat16 on the way count: a program that leaves them out, or rounds other values in their place, can miss the bound.
Values may be sent and summed in bfloat16 or wider, within the bound.
A program may use at most 128 MiB of HBM per device.

v0:
```python
import jax
import jax.numpy as jnp
from jax import lax
from jax.sharding import PartitionSpec as P

norm_eps = 1e-06
gate_band = 0.1
sparsity_coef = 0.05


def contract_first(left, right):
    return lax.dot_general(
        left, right, (((0,), (0,)), ((), ())), preferred_element_type=jnp.float32
    )


def local(
    residual_in, pre_gain, post_gain, w_gate, w_up, w_down, w_enc, b_enc, threshold, w_dec, b_dec
):
    full_rows = lax.all_gather(residual_in, "mp", axis=1, tiled=True)
    resid_wide = full_rows.astype(jnp.float32)
    normed = (
        resid_wide
        * lax.rsqrt(jnp.mean(resid_wide * resid_wide, axis=1, keepdims=True) + norm_eps)
        * pre_gain[None, :]
    ).astype(jnp.bfloat16)
    gate_out = jnp.dot(normed, w_gate, preferred_element_type=jnp.float32)
    up_out = jnp.dot(normed, w_up, preferred_element_type=jnp.float32)
    hidden = (jax.nn.gelu(gate_out, approximate=True) * up_out).astype(jnp.bfloat16)
    col_width = residual_in.shape[1]
    model_width = full_rows.shape[1]
    out_share = lax.psum_scatter(
        lax.dot_general(
            w_down, hidden, (((0,), (1,)), ((), ())), preferred_element_type=jnp.float32
        ),
        "mp",
        scatter_dimension=0,
        tiled=True,
    )
    total_sq = lax.psum(jnp.sum(out_share * out_share, axis=0), "mp")
    row_scale = lax.rsqrt(total_sq / model_width + norm_eps)
    my_cols = lax.axis_index("mp") * col_width
    gain_share = lax.dynamic_slice_in_dim(post_gain, my_cols, col_width, 0)
    mixed = residual_in.T.astype(jnp.float32) + out_share * row_scale[None, :] * gain_share[:, None]
    column_rows = lax.all_gather(mixed.astype(jnp.bfloat16), "mp", axis=0, tiled=True)
    h_cols = lax.all_gather(column_rows, "dp", axis=1, tiled=True)
    pre_act = contract_first(h_cols, w_enc) + b_enc[None, :]
    soft = jax.nn.sigmoid((pre_act - threshold[None, :]) / gate_band)
    feat_bf = (pre_act * soft).astype(jnp.bfloat16)
    gate_part = jnp.sum(soft)
    recon_part = lax.dot_general(
        w_dec, feat_bf, (((0,), (1,)), ((), ())), preferred_element_type=jnp.float32
    )
    recon_all, gate_total = lax.psum((recon_part, gate_part), ("dp", "mp"))
    error_t = recon_all + b_dec[:, None] - h_cols.astype(jnp.float32)
    grad_bdec = jnp.sum(error_t, axis=1)
    square_total = jnp.sum(error_t * error_t)
    err_bf = error_t.astype(jnp.bfloat16)
    loss_value = (0.5 * square_total + sparsity_coef * gate_total) / (
        h_cols.shape[0] * h_cols.shape[1]
    )
    grad_wdec = lax.dot_general(
        feat_bf, err_bf, (((0,), (1,)), ((), ())), preferred_element_type=jnp.float32
    ).astype(jnp.bfloat16)
    grad_feat = lax.dot_general(
        err_bf, w_dec, (((0,), (1,)), ((), ())), preferred_element_type=jnp.float32
    )
    slope = soft * (1.0 - soft) / gate_band
    side_term = (grad_feat * pre_act + sparsity_coef) * slope
    grad_pre = grad_feat * soft + side_term
    grad_thresh = -jnp.sum(side_term, axis=0)
    grad_benc = jnp.sum(grad_pre, axis=0)
    grad_wenc = jnp.dot(
        h_cols, grad_pre.astype(jnp.bfloat16), preferred_element_type=jnp.float32
    ).astype(jnp.bfloat16)
    return (loss_value, grad_wenc, grad_wdec, grad_benc, grad_thresh, grad_bdec)


def solution(mesh):
    placed = (
        P("dp", "mp"),
        P(),
        P(),
        P(None, "mp"),
        P(None, "mp"),
        P("mp", None),
        P(None, ("dp", "mp")),
        P(("dp", "mp")),
        P(("dp", "mp")),
        P(("dp", "mp"), None),
        P(),
    )
    return jax.shard_map(
        local,
        mesh=mesh,
        in_specs=placed,
        out_specs=(
            P(),
            P(None, ("dp", "mp")),
            P(("dp", "mp"), None),
            P(("dp", "mp")),
            P(("dp", "mp")),
            P(),
        ),
        check_vma=False,
    )
```

profile of v0, /device:TPU:1, one launch (start us, length us, event | category | flops | bytes accessed | tf_op | source)
XLA Modules:
  0.0 526.1 jit_solution(124205612583446622)
XLA Ops:
  7.2 27.9 %all_gather.9 = bf16[128,3584]{0,1:T(8,128)(2,1)S(1)} all-gather(bf16[128,112]{0,1:T(8,128)(2,1)} %param.11), channel_id=1, replica_groups=mesh['dp'=4,'mp'=32] {'mp'}, dimensions={1}, use_global_device_ids=true | all-gather | bytes 946176 | tf_op jit(solution)/shard_map/all_gather | solution.py:20
  35.1 0.5 fusion.2
  35.6 0.4 copy-done.1
  36.0 3.1 fusion.20
  39.1 6.0 %convolution_bitcast_fusion.1 = f32[3584,128]{0,1:T(8,128)} fusion(bf16[448,3584]{1,0:T(8,128)(2,1)S(1)} %copy-done, f32[128,448]{0,1:T(8,128)S(1)} %fusion.20, bf16[3584,448]{0,1:T(8,128)(2,1)} %param.15, bf16[128,3584]{0,1:T(8,128)(2,1)} %copy-done.1, f32[3584]{0:T(1024)S(1)} %copy-done.3, f32[128]{0:T(128)S(1)} %add_rsqrt_fusion.1), kind=kOutput, calls=%fused_computation.5 | convolution fusion | flops 824033280 | bytes 9419264 | tf_op jit(solution)/shard_map/dot_general | solution.py:33
  45.1 2.7 copy.23
  47.9 0.8 dynamic_slice.3
  48.6 75.3 %reduce-scatter.4.cloned.1.call-done = f32[112,128]{1,0:T(8,128)} async-done(((f32[3584,128]{1,0:T(8,128)}), f32[112,128]{1,0:T(8,128)}) %reduce-scatter.4.cloned.1.call-update) | async-done | bytes 57360 | tf_op jit(solution)/shard_map/reduce_scatter | solution.py:32
  123.9 0.9 copy.24
  124.9 64.3 %psum.21 = f32[128]{0:T(128)S(1)} all-reduce(f32[128]{0:T(128)S(1)} %multiply_reduce_fusion.1), channel_id=1, replica_groups=mesh['dp'=4,'mp'=32] {'mp'}, use_global_device_ids=true, to_apply=%region_3.0 | all-reduce | flops 128 | bytes 1024 | tf_op jit(solution)/shard_map/psum | solution.py:40
  189.3 0.9 fusion.23
  190.2 25.7 %all_gather.10 = bf16[3584,128]{1,0:T(8,128)(2,1)} all-gather(bf16[112,128]{1,0:T(8,128)(2,1)S(1)} %fusion.23), channel_id=1, replica_groups=mesh['dp'=4,'mp'=32] {'mp'}, dimensions={0}, use_global_device_ids=true | all-gather | bytes 946176 | tf_op jit(solution)/shard_map/all_gather | solution.py:45
  215.9 2.2 copy.22
  218.3 42.6 %all-gather.2.cloned.1.call-done = bf16[3584,512]{0,1:T(8,128)(2,1)} async-done(((bf16[3584,128]{0,1:T(8,128)(2,1)}), bf16[3584,512]{0,1:T(8,128)(2,1)}) %all-gather.2.cloned.1.call-update) | async-done | bytes 3670032 | tf_op jit(solution)/shard_map/all_gather | solution.py:46
  260.9 5.3 %convolution_add_fusion = f32[512,512]{1,0:T(8,128)S(1)} fusion(bf16[3584,512]{0,1:T(8,128)(2,1)} %all-gather.2.cloned.1.call-done, bf16[3584,512]{1,0:T(8,128)(2,1)} %param.17, f32[512]{0:T(512)S(1)} %copy-done.7), kind=kOutput, calls=%fused_computation.14 | convolution fusion | flops 1879310336 | bytes 8390656 | tf_op jit(solution)/shard_map/dot_general | solution.py:12
  266.3 1.0 copy-done.9
  267.2 5.1 convolution_bitcast_fusion
  272.4 160.2 %all-reduce.2.cloned.1.call-done = f32[3584,512]{0,1:T(8,128)} async-done(((f32[3584,512]{0,1:T(8,128)}), f32[3584,512]{0,1:T(8,128)}) %all-reduce.2.cloned.1.call-update) | async-done | bytes 7340048 | tf_op jit(solution)/shard_map/psum | solution.py:54
  432.6 5.9 %fusion = (f32[3584]{0:T(1024)}, f32[]{:T(128)}, bf16[3584,512]{0,1:T(8,128)(2,1)S(1)}) fusion(bf16[3584,512]{0,1:T(8,128)(2,1)} %all-gather.2.cloned.1.call-done, f32[3584,512]{0,1:T(8,128)} %all-reduce.2.cloned.1.call-done, f32[3584]{0:T(1024)S(1)} %copy-done.4), kind=kLoop, calls=%fused_computation.8 | loop fusion | flops 12841471 | bytes 14708740 | tf_op jit(solution)/shard_map/reduce_sum | solution.py:56
  438.6 3.9 fusion.25
  442.4 4.0 convolution_convert_fusion
  446.4 64.1 %psum.23 = f32[]{:T(128)} all-reduce(f32[]{:T(128)} %get-tuple-element.13), channel_id=1, replica_groups=mesh['dp'=4,'mp'=32] {'dp','mp'}, use_global_device_ids=true, to_apply=%region_7.0 | all-reduce | flops 1 | bytes 8 | tf_op jit(solution)/shard_map/psum | solution.py:54
  510.5 0.6 neg.7
  512.4 6.1 %convolution_convert_fusion.1 = bf16[3584,512]{1,0:T(8,128)(2,1)} fusion(bf16[3584,512]{0,1:T(8,128)(2,1)} %all-gather.2.cloned.1.call-done, bf16[512,512]{1,0:T(8,128)(2,1)} %get-tuple-element.11), kind=kOutput, calls=%fused_computation.4 | convolution fusion | flops 1880883200 | bytes 7864320 | tf_op jit(solution)/shard_map/dot_general | solution.py:73
  (29 shorter events, 0.5 us)
Async XLA Ops:
  7.2 31.9 %copy-start = (bf16[448,3584]{1,0:T(8,128)(2,1)S(1)}, bf16[448,3584]{1,0:T(8,128)(2,1)}, u32[]{:S(2)}) copy-start(bf16[448,3584]{1,0:T(8,128)(2,1)} %param.16) | copy-start | bytes 9633796
  7.2 116.7 %reduce-scatter.4.cloned.1.call-start = ((), (), s32[]{:S(2)}) async-start(), calls=%async_computation.3 | async-start | bytes 1892352 | tf_op jit(solution)/shard_map/reduce_scatter | solution.py:32
  35.1 0.9 copy-start.1
  35.1 4.0 copy-start.3
  45.1 144.2 %copy-start.2 = (bf16[128,112]{0,1:T(8,128)(2,1)S(1)}, bf16[128,112]{0,1:T(8,128)(2,1)}, u32[]{:S(2)}) copy-start(bf16[128,112]{0,1:T(8,128)(2,1)} %param.11) | copy-start | bytes 86020
  47.8 213.1 %copy-start.7 = (f32[512]{0:T(512)S(1)}, f32[512]{0:T(512)}, u32[]{:S(2)}) copy-start(f32[512]{0:T(512)} %param.18) | copy-start | bytes 6148
  47.8 213.1 %all-gather.2.cloned.1.call-start = ((), (), s32[]{:S(2)}) async-start(), calls=%async_computation.1 | async-start | bytes 4587520 | tf_op jit(solution)/shard_map/all_gather | solution.py:46
  218.1 49.1 %copy-start.8 = (f32[512]{0:T(512)S(1)}, f32[512]{0:T(512)}, u32[]{:S(2)}) copy-start(f32[512]{0:T(512)} %param.19) | copy-start | bytes 6148
  218.1 214.5 %all-reduce.2.cloned.1.call-start = ((), (), s32[]{:S(2)}) async-start(), calls=%async_computation.2 | async-start | bytes 14680064 | tf_op jit(solution)/shard_map/psum | solution.py:54
  260.9 6.3 %copy-start.5 = (bf16[512,3584]{1,0:T(8,128)(2,1)S(1)}, bf16[512,3584]{1,0:T(8,128)(2,1)}, u32[]{:S(2)}) copy-start(bf16[512,3584]{1,0:T(8,128)(2,1)} %param.20) | copy-start | bytes 11010052
  266.3 1.0 copy-start.9
  272.4 160.2 %copy-start.4 = (f32[3584]{0:T(1024)S(1)}, f32[3584]{0:T(1024)}, u32[]{:S(2)}) copy-start(f32[3584]{0:T(1024)} %param.21) | copy-start | bytes 43012
  432.6 6.0 %copy-start.6 = (bf16[512,3584]{1,0:T(8,128)(2,1)S(1)}, bf16[512,3584]{1,0:T(8,128)(2,1)}, u32[]{:S(2)}) copy-start(bf16[512,3584]{1,0:T(8,128)(2,1)} %param.20) | copy-start | bytes 11010052
  432.6 6.0 %copy-start.10 = (f32[512,512]{1,0:T(8,128)S(1)}, f32[512,512]{1,0:T(8,128)}, u32[]{:S(2)}) copy-start(f32[512,512]{1,0:T(8,128)} %copy-done.9) | copy-start | bytes 3145732
Sparse Core Ops, SparseCore 0:
  47.9 75.9 reduce-scatter.3
  218.2 42.6 all-gather.1
  272.5 160.0 all-reduce.1
where the time goes:
time: 527 us; the launch traced here: 526 us
  waiting for transfers between devices  278 us (53%)
  blocking collectives  182 us (35%)
  matrix products  33.4 us (6%)
  between operations  16.3 us (3%)
  local copies, waits for them, and re-layouts  8.05 us (2%)
  other arithmetic  8.04 us (2%)
    psum x1, waiting for transfers between devices, local(): recon_all, gate_total = lax.psum((recon_part, gate_part), ('dp', 'mp'))  160 us
    reduce_scatter x1, waiting for transfers between devices, local(): lax.psum_scatter(lax.dot_general(w_down, hidden, (((0,), (1,)), ((), ()))...  75.3 us
    psum x1, blocking collectives, local(): total_sq = lax.psum(jnp.sum(out_share * out_share, axis=0), 'mp')  64.3 us
    psum x1, blocking collectives, local(): recon_all, gate_total = lax.psum((recon_part, gate_part), ('dp', 'mp'))  64.1 us
    all_gather x1, waiting for transfers between devices, local(): h_cols = lax.all_gather(column_rows, 'dp', axis=1, tiled=True)  42.6 us
    all_gather x1, blocking collectives, local(): full_rows = lax.all_gather(residual_in, 'mp', axis=1, tiled=True)  27.9 us
    all_gather x1, blocking collectives, local(): lax.all_gather(mixed.astype(jnp.bfloat16), 'mp', axis=0, tiled=True)  25.7 us
  transfers between devices with their start and end apart: 3, of which 3 were waited for; matrix products, arithmetic and copies ran while one was open for 0% of the time, Pallas kernels for 0%

commit v1 on v0

--- a/solution.py
+++ b/solution.py
@@ -37,7 +37,9 @@
         scatter_dimension=0,
         tiled=True,
     )
-    total_sq = lax.psum(jnp.sum(out_share * out_share, axis=0), "mp")
+    z_in = jnp.sum(out_share * out_share, axis=0)
+    clean = lax.all_gather(z_in, axis_name="mp")
+    total_sq = jnp.sum(clean, axis=0)
     row_scale = lax.rsqrt(total_sq / model_width + norm_eps)
     my_cols = lax.axis_index("mp") * col_width
     gain_share = lax.dynamic_slice_in_dim(post_gain, my_cols, col_width, 0)

time: 527 us -> 485 us (0.920)
  blocking collectives: 182 us -> 140 us
    psum x1 -> x0, blocking collectives: 64.3 us -> none  [local(): total_sq = lax.psum(jnp.sum(out_share * out_share, axis=0), 'mp')]
    all_gather x0 -> x1, blocking collectives: none -> 22.6 us  [local(): clean = lax.all_gather(z_in, axis_name='mp')]
where the time goes in v1:
time: 485 us; the launch traced here: 484 us
  waiting for transfers between devices  278 us (57%)
  blocking collectives  140 us (29%)
  matrix products  33.4 us (7%)
  between operations  16.3 us (3%)
  other arithmetic  8.09 us (2%)
  local copies, waits for them, and re-layouts  8.05 us (2%)
    psum x1, waiting for transfers between devices, local(): recon_all, gate_total = lax.psum((recon_part, gate_part), ('dp', 'mp'))  160 us
    reduce_scatter x1, waiting for transfers between devices, local(): lax.psum_scatter(lax.dot_general(w_down, hidden, (((0,), (1,)), ((), ()))...  75.3 us
    psum x1, blocking collectives, local(): recon_all, gate_total = lax.psum((recon_part, gate_part), ('dp', 'mp'))  64.1 us
    all_gather x1, waiting for transfers between devices, local(): h_cols = lax.all_gather(column_rows, 'dp', axis=1, tiled=True)  43 us
    all_gather x1, blocking collectives, local(): full_rows = lax.all_gather(residual_in, 'mp', axis=1, tiled=True)  27.9 us
    all_gather x1, blocking collectives, local(): lax.all_gather(mixed.astype(jnp.bfloat16), 'mp', axis=0, tiled=True)  25.2 us
    all_gather x1, blocking collectives, local(): clean = lax.all_gather(z_in, axis_name='mp')  22.6 us
  transfers between devices with their start and end apart: 3, of which 3 were waited for; matrix products, arithmetic and copies ran while one was open for 0% of the time, Pallas kernels for 0%

profile of v1, /device:TPU:1, one launch (start us, length us, event | category | flops | bytes accessed | tf_op | source)
XLA Modules:
  0.0 484.2 jit_solution(3020985249148445307)
XLA Ops:
  7.2 27.9 %all_gather.15 = bf16[128,3584]{0,1:T(8,128)(2,1)S(1)} all-gather(bf16[128,112]{0,1:T(8,128)(2,1)} %param.11), channel_id=1, replica_groups=mesh['dp'=4,'mp'=32] {'mp'}, dimensions={1}, use_global_device_ids=true | all-gather | bytes 946176 | tf_op jit(solution)/shard_map/all_gather | solution.py:20
  35.1 0.5 fusion.2
  35.6 0.4 copy-done.1
  36.0 3.1 fusion.20
  39.1 6.0 %convolution_bitcast_fusion.1 = f32[3584,128]{0,1:T(8,128)} fusion(bf16[448,3584]{1,0:T(8,128)(2,1)S(1)} %copy-done, f32[128,448]{0,1:T(8,128)S(1)} %fusion.20, bf16[3584,448]{0,1:T(8,128)(2,1)} %param.15, bf16[128,3584]{0,1:T(8,128)(2,1)} %copy-done.1, f32[3584]{0:T(1024)S(1)} %copy-done.3, f32[128]{0:T(128)S(1)} %add_rsqrt_fusion.1), kind=kOutput, calls=%fused_computation.5 | convolution fusion | flops 824033280 | bytes 9419264 | tf_op jit(solution)/shard_map/dot_general | solution.py:33
  45.1 2.7 copy.23
  47.9 0.8 dynamic_slice.3
  48.6 75.3 %reduce-scatter.4.cloned.1.call-done = f32[112,128]{1,0:T(8,128)} async-done(((f32[3584,128]{1,0:T(8,128)}), f32[112,128]{1,0:T(8,128)}) %reduce-scatter.4.cloned.1.call-update) | async-done | bytes 57360 | tf_op jit(solution)/shard_map/reduce_scatter | solution.py:32
  123.9 0.9 copy.24
  124.9 22.6 %all-gather.1 = f32[32,1,128]{2,1,0:T(1,128)S(1)} all-gather(f32[1,1,128]{2,1,0:T(1,128)S(1)} %bitcast.21), channel_id=2, replica_groups=mesh['dp'=4,'mp'=32] {'mp'}, dimensions={0}, use_global_device_ids=true | all-gather | bytes 16896 | tf_op jit(solution)/shard_map/all_gather | solution.py:41
  147.6 0.9 fusion.23
  148.5 25.2 %all_gather.18 = bf16[3584,128]{1,0:T(8,128)(2,1)} all-gather(bf16[112,128]{1,0:T(8,128)(2,1)S(1)} %fusion.23), channel_id=1, replica_groups=mesh['dp'=4,'mp'=32] {'mp'}, dimensions={0}, use_global_device_ids=true | all-gather | bytes 946176 | tf_op jit(solution)/shard_map/all_gather | solution.py:47
  173.7 2.2 copy.22
  176.1 43.0 %all-gather.4.cloned.1.call-done = bf16[3584,512]{0,1:T(8,128)(2,1)} async-done(((bf16[3584,128]{0,1:T(8,128)(2,1)}), bf16[3584,512]{0,1:T(8,128)(2,1)}) %all-gather.4.cloned.1.call-update) | async-done | bytes 3670032 | tf_op jit(solution)/shard_map/all_gather | solution.py:48
  219.1 5.3 %convolution_add_fusion = f32[512,512]{1,0:T(8,128)S(1)} fusion(bf16[3584,512]{0,1:T(8,128)(2,1)} %all-gather.4.cloned.1.call-done, bf16[3584,512]{1,0:T(8,128)(2,1)} %param.17, f32[512]{0:T(512)S(1)} %copy-done.7), kind=kOutput, calls=%fused_computation.14 | convolution fusion | flops 1879310336 | bytes 8390656 | tf_op jit(solution)/shard_map/dot_general | solution.py:12
  224.5 1.0 copy-done.9
  225.5 5.2 %convolution_bitcast_fusion = f32[3584,512]{0,1:T(8,128)} fusion(bf16[512,3584]{1,0:T(8,128)(2,1)S(1)} %copy-done.5, f32[512,512]{1,0:T(8,128)S(1)} %convolution_add_fusion, f32[512]{0:T(512)S(1)} %copy-done.8), kind=kOutput, calls=%fused_computation.2 | convolution fusion | flops 1880883200 | bytes 12060672 | tf_op jit(solution)/shard_map/dot_general | solution.py:53
  230.6 160.1 %all-reduce.2.cloned.1.call-done = f32[3584,512]{0,1:T(8,128)} async-done(((f32[3584,512]{0,1:T(8,128)}), f32[3584,512]{0,1:T(8,128)}) %all-reduce.2.cloned.1.call-update) | async-done | bytes 7340048 | tf_op jit(solution)/shard_map/psum | solution.py:56
  390.8 5.9 %fusion = (f32[3584]{0:T(1024)}, f32[]{:T(128)}, bf16[3584,512]{0,1:T(8,128)(2,1)S(1)}) fusion(bf16[3584,512]{0,1:T(8,128)(2,1)} %all-gather.4.cloned.1.call-done, f32[3584,512]{0,1:T(8,128)} %all-reduce.2.cloned.1.call-done, f32[3584]{0:T(1024)S(1)} %copy-done.4), kind=kLoop, calls=%fused_computation.8 | loop fusion | flops 12841471 | bytes 14708740 | tf_op jit(solution)/shard_map/reduce_sum | solution.py:58
  396.7 3.9 fusion.25
  400.6 4.0 convolution_convert_fusion
  404.6 64.1 %psum.15 = f32[]{:T(128)} all-reduce(f32[]{:T(128)} %get-tuple-element.13), channel_id=1, replica_groups=mesh['dp'=4,'mp'=32] {'dp','mp'}, use_global_device_ids=true, to_apply=%region_7.0 | all-reduce | flops 1 | bytes 8 | tf_op jit(solution)/shard_map/psum | solution.py:56
  468.6 0.6 neg.7
  470.5 6.1 %convolution_convert_fusion.1 = bf16[3584,512]{1,0:T(8,128)(2,1)} fusion(bf16[3584,512]{0,1:T(8,128)(2,1)} %all-gather.4.cloned.1.call-done, bf16[512,512]{1,0:T(8,128)(2,1)} %get-tuple-element.11), kind=kOutput, calls=%fused_computation.4 | convolution fusion | flops 1880883200 | bytes 7864320 | tf_op jit(solution)/shard_map/dot_general | solution.py:75
  (30 shorter events, 0.6 us)
Async XLA Ops:
  7.2 31.9 %copy-start = (bf16[448,3584]{1,0:T(8,128)(2,1)S(1)}, bf16[448,3584]{1,0:T(8,128)(2,1)}, u32[]{:S(2)}) copy-start(bf16[448,3584]{1,0:T(8,128)(2,1)} %param.16) | copy-start | bytes 9633796
  7.2 116.7 %reduce-scatter.4.cloned.1.call-start = ((), (), s32[]{:S(2)}) async-start(), calls=%async_computation.3 | async-start | bytes 1892352 | tf_op jit(solution)/shard_map/reduce_scatter | solution.py:32
  35.1 0.9 copy-start.1
  35.1 4.0 copy-start.3
  45.1 102.5 %copy-start.2 = (bf16[128,112]{0,1:T(8,128)(2,1)S(1)}, bf16[128,112]{0,1:T(8,128)(2,1)}, u32[]{:S(2)}) copy-start(bf16[128,112]{0,1:T(8,128)(2,1)} %param.11) | copy-start | bytes 86020
  47.8 171.3 %copy-start.7 = (f32[512]{0:T(512)S(1)}, f32[512]{0:T(512)}, u32[]{:S(2)}) copy-start(f32[512]{0:T(512)} %param.18) | copy-start | bytes 6148
  47.8 171.3 %all-gather.4.cloned.1.call-start = ((), (), s32[]{:S(2)}) async-start(), calls=%async_computation.1 | async-start | bytes 4587520 | tf_op jit(solution)/shard_map/all_gather | solution.py:48
  175.9 49.5 %copy-start.8 = (f32[512]{0:T(512)S(1)}, f32[512]{0:T(512)}, u32[]{:S(2)}) copy-start(f32[512]{0:T(512)} %param.19) | copy-start | bytes 6148
  175.9 214.8 %all-reduce.2.cloned.1.call-start = ((), (), s32[]{:S(2)}) async-start(), calls=%async_computation.2 | async-start | bytes 14680064 | tf_op jit(solution)/shard_map/psum | solution.py:56
  219.1 6.3 %copy-start.5 = (bf16[512,3584]{1,0:T(8,128)(2,1)S(1)}, bf16[512,3584]{1,0:T(8,128)(2,1)}, u32[]{:S(2)}) copy-start(bf16[512,3584]{1,0:T(8,128)(2,1)} %param.20) | copy-start | bytes 11010052
  224.5 1.0 copy-start.9
  230.6 160.1 %copy-start.4 = (f32[3584]{0:T(1024)S(1)}, f32[3584]{0:T(1024)}, u32[]{:S(2)}) copy-start(f32[3584]{0:T(1024)} %param.21) | copy-start | bytes 43012
  390.8 6.0 %copy-start.6 = (bf16[512,3584]{1,0:T(8,128)(2,1)S(1)}, bf16[512,3584]{1,0:T(8,128)(2,1)}, u32[]{:S(2)}) copy-start(bf16[512,3584]{1,0:T(8,128)(2,1)} %param.20) | copy-start | bytes 11010052
  390.8 6.0 %copy-start.10 = (f32[512,512]{1,0:T(8,128)S(1)}, f32[512,512]{1,0:T(8,128)}, u32[]{:S(2)}) copy-start(f32[512,512]{1,0:T(8,128)} %copy-done.9) | copy-start | bytes 3145732
Sparse Core Ops, SparseCore 0:
  47.9 75.9 reduce-scatter.3
  176.0 43.0 all-gather.3
  230.8 159.9 all-reduce.1
